TPU v7x, 32 devices: a whole 2x2x4 slice. The times are simulated.
32 devices in a mesh: tgt: 4 (over y, core), src: 8 (over z, x).
Axes of the slice: x: 2, y: 2, z: 4, core: 2. Of those that a mesh axis runs over, the one named last changes fastest.
Arguments:
- targets: bfloat16 [16, 64, 4096], P('tgt', 'src'), may hold values from -6 to 6
- sources: bfloat16 [8, 64, 4096], P('src', 'tgt'), may hold values from -6 to 6
- exponents: float32 [8], replicated, may hold values from 0.005 to 0.76
- coefficients: float32 [8], replicated, may hold values from -0.08 to 0.08
Outputs:
- exchange: float32 [64, 16, 4096], P('src', 'tgt')
All inputs are finite; a program needn't handle non-finite values.
Results may differ from a plain program's by a relative error of at most 0.0063.
The roundings to bfloat16 on the way count: a program that leaves them out, or rounds other values in their place, can miss the bound.
Values may be sent and summed in bfloat16 or wider, within the bound.
A program may use at most 64 MiB of HBM per device.

v0:
```python
import jax
import jax.numpy as jnp
from jax import lax
from jax.sharding import PartitionSpec as P

G = 64


def passed_along(value, axis, steps):
    count = lax.axis_size(axis)
    pairs = [(source, (source + steps) % count) for source in range(count)]
    return lax.ppermute(value, axis, pairs)


def kernels(exponents, coefficients):
    grid_pos = jnp.arange(G, dtype=jnp.int32)
    distance = jnp.abs(grid_pos[:, None] - grid_pos[None, :])
    distance = jnp.minimum(distance, G - distance).astype(jnp.float32)
    gauss_table = jnp.exp(-exponents[:, None, None] * (distance * distance)[None])
    weighted = coefficients[:, None, None] * gauss_table
    return (gauss_table.astype(jnp.bfloat16), weighted.astype(jnp.bfloat16))


def slab_terms(targets_full, source_block, kernel_table, weighted, row_start, row_count):
    kernel_rows = lax.dynamic_slice_in_dim(kernel_table, row_start, row_count, 1)
    target_count = targets_full.shape[0]
    source_count = source_block.shape[0]
    side_len = targets_full.shape[1]
    term_count = kernel_table.shape[0]

    def over_targets(target_index, summed):
        target = lax.dynamic_index_in_dim(targets_full, target_index, 0, keepdims=False)

        def over_sources(source_index, partial_value):
            source = lax.dynamic_index_in_dim(source_block, source_index, 0, keepdims=False)
            density = (target.astype(jnp.float32) * source.astype(jnp.float32)).astype(jnp.bfloat16)
            first_pass = jnp.einsum(
                "gax,xm->gam", kernel_rows, density, preferred_element_type=jnp.float32
            ).astype(jnp.bfloat16)
            first_pass = first_pass.reshape(term_count, row_count, side_len, side_len)
            second_pass = jnp.einsum(
                "gby,gayz->gabz", kernel_table, first_pass, preferred_element_type=jnp.float32
            ).astype(jnp.bfloat16)
            potential = jnp.einsum(
                "gcz,gabz->abc", weighted, second_pass, preferred_element_type=jnp.float32
            ).reshape(row_count, side_len * side_len)
            source_rows = lax.dynamic_slice_in_dim(source, row_start, row_count, 0).astype(
                jnp.float32
            )
            return partial_value + potential * source_rows

        partial_value = lax.fori_loop(
            0, source_count, over_sources, jnp.zeros((row_count, side_len * side_len), jnp.float32)
        )
        return lax.dynamic_update_slice_in_dim(summed, partial_value[:, None, :], target_index, 1)

    return lax.fori_loop(
        0,
        target_count,
        over_targets,
        jnp.zeros((row_count, target_count, side_len * side_len), jnp.float32),
    )


def shards(targets, sources, exponents, coefficients):
    kernel_table, weighted = kernels(exponents, coefficients)
    targets_full = lax.all_gather(targets, "src", axis=1, tiled=True)
    sources_full = lax.all_gather(sources, "tgt", axis=1, tiled=True)
    planes = targets.shape[1]
    side_len = targets_full.shape[1]
    target_count = targets_full.shape[0]
    row_start = lax.axis_index("src") * planes

    def cycle_turn(turn_index, cycle_state):
        source_block, summed = cycle_state
        summed = summed + slab_terms(
            targets_full, source_block, kernel_table, weighted, row_start, planes
        )
        source_block = passed_along(source_block, "src", 1)
        return (source_block, summed)

    start_sum = jnp.zeros((planes, target_count, side_len * side_len), jnp.float32)
    source_block, summed = lax.fori_loop(
        0, lax.axis_size("src") - 1, cycle_turn, (sources_full, start_sum)
    )
    owned_part = summed + slab_terms(
        targets_full, source_block, kernel_table, weighted, row_start, planes
    )
    return -owned_part


def solution(mesh):
    placed = (P("tgt", "src", None), P("src", "tgt", None), P(), P())
    return jax.shard_map(
        shards, mesh=mesh, in_specs=placed, out_specs=P("src", "tgt", None), check_vma=False
    )
```

profile of v0, /device:TPU:0, one launch (start us, length us, event | category | flops | bytes accessed | tf_op | source)
XLA Modules:
  0.0 222.8 jit_solution(5835023741297192514)
XLA Ops:
  8.0 8.9 %all_gather.6 = bf16[1,64,4096]{2,1,0:T(8,128)(2,1)S(1)} all-gather(bf16[1,16,4096]{2,1,0:T(8,128)(2,1)} %param.11), channel_id=1, replica_groups=mesh['tgt'=4,'src'=8] {'tgt'}, dimensions={1}, use_global_device_ids=true | all-gather | bytes 655360 | tf_op jit(solution)/shard_map/all_gather | solution.py:68
  16.9 44.6 %all-gather.2.cloned.1.call-done = bf16[4,64,4096]{2,1,0:T(8,128)(2,1)} async-done(((bf16[4,8,4096]{2,1,0:T(8,128)(2,1)}), bf16[4,64,4096]{2,1,0:T(8,128)(2,1)}) %all-gather.2.cloned.1.call-update) | async-done | bytes 2097168 | tf_op jit(solution)/shard_map/all_gather | solution.py:67
  61.5 124.2 %while.87 = (s32[]{:T(128)}, bf16[1,64,4096]{2,1,0:T(8,128)(2,1)S(1)}, f32[8,4,4096]{2,0,1:T(8,128)S(1)}, s32[]{:T(128)}, bf16[4,64,4096]{2,1,0:T(8,128)(2,1)}, ...) while((s32[]{:T(128)}, ...), condition=%wide.region_3.0_spmd.clone.clone.clone.clone, body=%wide.region_0.3_spmd.clone.clone.clone.sunk.clone | while | flops 102694912 | bytes 9003932 | solution.py:83
  64.6 14.0 %while.86 = (s32[]{:T(128)}, f32[8,4,4096]{2,0,1:T(8,128)S(1)}, bf16[4,64,4096]{2,1,0:T(8,128)(2,1)}, bf16[1,64,4096]{2,1,0:T(8,128)(2,1)}, bf16[8,8,64]{2,1,0:T...) while((s32[]{:T(128)}, f32[8,4,4096]{2,0,1:T(8,128)S(1)}, ...), condition=%wide.region_2.2_spmd, body=%wide.region_1.1_spmd.sunk | while | flops 102301696 | bytes 4006497 | solution.py:57
  64.6 1.5 fusion.76
  68.1 1.5 fusion.76
  71.6 1.5 fusion.76
  75.1 1.5 fusion.76
  79.5 2.4 %collective-permute-start = (bf16[1,64,4096]{2,1,0:T(8,128)(2,1)}, bf16[1,64,4096]{2,1,0:T(8,128)(2,1)S(1)}, u32[]{:S(2)}, u32[]{:S(2)}) collective-permute-start(bf16[1,64,4096]{2,1,0:T(8,128)(2,1)} %copy.42), channel_id=1, source_target_pairs={{0,1},{1,2},{2,3},{3,4},{4,5},{5,6},{6,7},{7,0},{8,9},{9,10},{10,1... | collective-permute-start | bytes 1572872 | tf_op jit(solution)/shard_map/while/body/eval_jaxpr/ppermute | solution.py:12
  83.6 13.9 %while.86 = (s32[]{:T(128)}, f32[8,4,4096]{2,0,1:T(8,128)S(1)}, bf16[4,64,4096]{2,1,0:T(8,128)(2,1)}, bf16[1,64,4096]{2,1,0:T(8,128)(2,1)}, bf16[8,8,64]{2,1,0:T...) while((s32[]{:T(128)}, f32[8,4,4096]{2,0,1:T(8,128)S(1)}, ...), condition=%wide.region_2.2_spmd, body=%wide.region_1.1_spmd.sunk | while | flops 102301696 | bytes 4006497 | solution.py:57
  83.6 1.5 fusion.76
  87.1 1.5 fusion.76
  90.6 1.5 fusion.76
  94.1 1.5 fusion.76
  100.8 13.9 %while.86 = (s32[]{:T(128)}, f32[8,4,4096]{2,0,1:T(8,128)S(1)}, bf16[4,64,4096]{2,1,0:T(8,128)(2,1)}, bf16[1,64,4096]{2,1,0:T(8,128)(2,1)}, bf16[8,8,64]{2,1,0:T...) while((s32[]{:T(128)}, f32[8,4,4096]{2,0,1:T(8,128)S(1)}, ...), condition=%wide.region_2.2_spmd, body=%wide.region_1.1_spmd.sunk | while | flops 102301696 | bytes 4006497 | solution.py:57
  100.8 1.5 fusion.76
  104.3 1.5 fusion.76
  107.7 1.5 fusion.76
  111.2 1.5 fusion.76
  115.7 1.8 collective-permute-start
  119.2 13.9 %while.86 = (s32[]{:T(128)}, f32[8,4,4096]{2,0,1:T(8,128)S(1)}, bf16[4,64,4096]{2,1,0:T(8,128)(2,1)}, bf16[1,64,4096]{2,1,0:T(8,128)(2,1)}, bf16[8,8,64]{2,1,0:T...) while((s32[]{:T(128)}, f32[8,4,4096]{2,0,1:T(8,128)S(1)}, ...), condition=%wide.region_2.2_spmd, body=%wide.region_1.1_spmd.sunk | while | flops 102301696 | bytes 4006497 | solution.py:57
  119.2 1.5 fusion.76
  122.7 1.5 fusion.76
  126.2 1.5 fusion.76
  129.6 1.5 fusion.76
  136.3 13.9 %while.86 = (s32[]{:T(128)}, f32[8,4,4096]{2,0,1:T(8,128)S(1)}, bf16[4,64,4096]{2,1,0:T(8,128)(2,1)}, bf16[1,64,4096]{2,1,0:T(8,128)(2,1)}, bf16[8,8,64]{2,1,0:T...) while((s32[]{:T(128)}, f32[8,4,4096]{2,0,1:T(8,128)S(1)}, ...), condition=%wide.region_2.2_spmd, body=%wide.region_1.1_spmd.sunk | while | flops 102301696 | bytes 4006497 | solution.py:57
  136.4 1.5 fusion.76
  139.8 1.5 fusion.76
  143.3 1.5 fusion.76
  146.8 1.5 fusion.76
  151.3 1.5 collective-permute-start
  154.4 13.9 %while.86 = (s32[]{:T(128)}, f32[8,4,4096]{2,0,1:T(8,128)S(1)}, bf16[4,64,4096]{2,1,0:T(8,128)(2,1)}, bf16[1,64,4096]{2,1,0:T(8,128)(2,1)}, bf16[8,8,64]{2,1,0:T...) while((s32[]{:T(128)}, f32[8,4,4096]{2,0,1:T(8,128)S(1)}, ...), condition=%wide.region_2.2_spmd, body=%wide.region_1.1_spmd.sunk | while | flops 102301696 | bytes 4006497 | solution.py:57
  154.4 1.5 fusion.76
  157.9 1.5 fusion.76
  161.4 1.5 fusion.76
  164.9 1.5 fusion.76
  171.6 13.9 %while.86 = (s32[]{:T(128)}, f32[8,4,4096]{2,0,1:T(8,128)S(1)}, bf16[4,64,4096]{2,1,0:T(8,128)(2,1)}, bf16[1,64,4096]{2,1,0:T(8,128)(2,1)}, bf16[8,8,64]{2,1,0:T...) while((s32[]{:T(128)}, f32[8,4,4096]{2,0,1:T(8,128)S(1)}, ...), condition=%wide.region_2.2_spmd, body=%wide.region_1.1_spmd.sunk | while | flops 102301696 | bytes 4006497 | solution.py:57
  171.6 1.5 fusion.76
  175.1 1.5 fusion.76
  178.6 1.5 fusion.76
  182.1 1.5 fusion.76
  185.7 28.0 %while.85 = (s32[]{:T(128)}, f32[8,4,4096]{2,1,0:T(4,128)}, bf16[4,64,4096]{2,1,0:T(8,128)(2,1)}, bf16[1,64,4096]{2,1,0:T(8,128)(2,1)S(1)}, bf16[8,8,64]{2,1,0:T...) while((s32[]{:T(128)}, f32[8,4,4096]{2,1,0:T(4,128)}, ...), condition=%wide.region_5.6_spmd.clone.clone.clone, body=%wide.region_4.5_spmd.clone.clone.sunk.clone | while | flops 102465536 | bytes 4416317 | solution.py:57
  189.3 3.4 %dynamic_update_slice.25 = f32[8,4,4096]{2,1,0:T(4,128)} dynamic-update-slice(f32[8,4,4096]{2,1,0:T(4,128)} %get-tuple-element.1175, f32[8,1,4096]{2,1,0:T(1,128)S(1)} %copy.29, s32[]{:T(128)} %constant.171.clone.1..sunk.2, s32[]{:T(128)} %get-tuple-element.1174, s32[]{:T(128)} %constant.171.clone.1..sunk.2) | dynamic-update-slice | bytes 262148 | tf_op jit(solution)/shard_map/while/body/eval_jaxpr/dynamic_update_slice | solution.py:55
  192.7 1.3 fusion.84
  196.3 3.4 %dynamic_update_slice.25 = f32[8,4,4096]{2,1,0:T(4,128)} dynamic-update-slice(f32[8,4,4096]{2,1,0:T(4,128)} %get-tuple-element.1175, f32[8,1,4096]{2,1,0:T(1,128)S(1)} %copy.29, s32[]{:T(128)} %constant.171.clone.1..sunk.2, s32[]{:T(128)} %get-tuple-element.1174, s32[]{:T(128)} %constant.171.clone.1..sunk.2) | dynamic-update-slice | bytes 262148 | tf_op jit(solution)/shard_map/while/body/eval_jaxpr/dynamic_update_slice | solution.py:55
  203.3 3.4 %dynamic_update_slice.25 = f32[8,4,4096]{2,1,0:T(4,128)} dynamic-update-slice(f32[8,4,4096]{2,1,0:T(4,128)} %get-tuple-element.1175, f32[8,1,4096]{2,1,0:T(1,128)S(1)} %copy.29, s32[]{:T(128)} %constant.171.clone.1..sunk.2, s32[]{:T(128)} %get-tuple-element.1174, s32[]{:T(128)} %constant.171.clone.1..sunk.2) | dynamic-update-slice | bytes 262148 | tf_op jit(solution)/shard_map/while/body/eval_jaxpr/dynamic_update_slice | solution.py:55
  210.3 3.4 %dynamic_update_slice.25 = f32[8,4,4096]{2,1,0:T(4,128)} dynamic-update-slice(f32[8,4,4096]{2,1,0:T(4,128)} %get-tuple-element.1175, f32[8,1,4096]{2,1,0:T(1,128)S(1)} %copy.29, s32[]{:T(128)} %constant.171.clone.1..sunk.2, s32[]{:T(128)} %get-tuple-element.1174, s32[]{:T(128)} %constant.171.clone.1..sunk.2) | dynamic-update-slice | bytes 262148 | tf_op jit(solution)/shard_map/while/body/eval_jaxpr/dynamic_update_slice | solution.py:55
  213.7 2.2 %fusion.44 = f32[8,4,4096]{2,1,0:T(4,128)} fusion(f32[8,4,4096]{2,1,0:T(4,128)} %get-tuple-element.660, f32[8,4,4096]{2,0,1:T(8,128)S(1)} %get-tuple-element.658), kind=kLoop, calls=%fused_computation.45 | loop fusion | flops 262144 | bytes 1572864 | tf_op jit(solution)/shard_map/neg | solution.py:89
  (198 shorter events, 89.4 us)
Async XLA Ops:
  6.5 55.0 %all-gather.2.cloned.1.call-start = ((), (), s32[]{:S(2)}) async-start(), calls=%async_computation | async-start | bytes 2359296 | tf_op jit(solution)/shard_map/all_gather | solution.py:67
  62.4 16.3 %collective-permute-start = (bf16[1,64,4096]{2,1,0:T(8,128)(2,1)}, bf16[1,64,4096]{2,1,0:T(8,128)(2,1)S(1)}, u32[]{:S(2)}, u32[]{:S(2)}) collective-permute-start(bf16[1,64,4096]{2,1,0:T(8,128)(2,1)} %copy.42), channel_id=1, source_target_pairs={{0,1},{1,2},{2,3},{3,4},{4,5},{5,6},{6,7},{7,0},{8,9},{9,10},{10,1... | collective-permute-start | bytes 1572872 | tf_op jit(solution)/shard_map/while/body/eval_jaxpr/ppermute | solution.py:12
  79.5 18.2 %collective-permute-start = (bf16[1,64,4096]{2,1,0:T(8,128)(2,1)}, bf16[1,64,4096]{2,1,0:T(8,128)(2,1)S(1)}, u32[]{:S(2)}, u32[]{:S(2)}) collective-permute-start(bf16[1,64,4096]{2,1,0:T(8,128)(2,1)} %copy.42), channel_id=1, source_target_pairs={{0,1},{1,2},{2,3},{3,4},{4,5},{5,6},{6,7},{7,0},{8,9},{9,10},{10,1... | collective-permute-start | bytes 1572872 | tf_op jit(solution)/shard_map/while/body/eval_jaxpr/ppermute | solution.py:12
  98.5 16.3 %collective-permute-start = (bf16[1,64,4096]{2,1,0:T(8,128)(2,1)}, bf16[1,64,4096]{2,1,0:T(8,128)(2,1)S(1)}, u32[]{:S(2)}, u32[]{:S(2)}) collective-permute-start(bf16[1,64,4096]{2,1,0:T(8,128)(2,1)} %copy.42), channel_id=1, source_target_pairs={{0,1},{1,2},{2,3},{3,4},{4,5},{5,6},{6,7},{7,0},{8,9},{9,10},{10,1... | collective-permute-start | bytes 1572872 | tf_op jit(solution)/shard_map/while/body/eval_jaxpr/ppermute | solution.py:12
  115.7 17.6 %collective-permute-start = (bf16[1,64,4096]{2,1,0:T(8,128)(2,1)}, bf16[1,64,4096]{2,1,0:T(8,128)(2,1)S(1)}, u32[]{:S(2)}, u32[]{:S(2)}) collective-permute-start(bf16[1,64,4096]{2,1,0:T(8,128)(2,1)} %copy.42), channel_id=1, source_target_pairs={{0,1},{1,2},{2,3},{3,4},{4,5},{5,6},{6,7},{7,0},{8,9},{9,10},{10,1... | collective-permute-start | bytes 1572872 | tf_op jit(solution)/shard_map/while/body/eval_jaxpr/ppermute | solution.py:12
  134.1 16.3 %collective-permute-start = (bf16[1,64,4096]{2,1,0:T(8,128)(2,1)}, bf16[1,64,4096]{2,1,0:T(8,128)(2,1)S(1)}, u32[]{:S(2)}, u32[]{:S(2)}) collective-permute-start(bf16[1,64,4096]{2,1,0:T(8,128)(2,1)} %copy.42), channel_id=1, source_target_pairs={{0,1},{1,2},{2,3},{3,4},{4,5},{5,6},{6,7},{7,0},{8,9},{9,10},{10,1... | collective-permute-start | bytes 1572872 | tf_op jit(solution)/shard_map/while/body/eval_jaxpr/ppermute | solution.py:12
  151.3 17.2 %collective-permute-start = (bf16[1,64,4096]{2,1,0:T(8,128)(2,1)}, bf16[1,64,4096]{2,1,0:T(8,128)(2,1)S(1)}, u32[]{:S(2)}, u32[]{:S(2)}) collective-permute-start(bf16[1,64,4096]{2,1,0:T(8,128)(2,1)} %copy.42), channel_id=1, source_target_pairs={{0,1},{1,2},{2,3},{3,4},{4,5},{5,6},{6,7},{7,0},{8,9},{9,10},{10,1... | collective-permute-start | bytes 1572872 | tf_op jit(solution)/shard_map/while/body/eval_jaxpr/ppermute | solution.py:12
  169.4 16.3 %collective-permute-start = (bf16[1,64,4096]{2,1,0:T(8,128)(2,1)}, bf16[1,64,4096]{2,1,0:T(8,128)(2,1)S(1)}, u32[]{:S(2)}, u32[]{:S(2)}) collective-permute-start(bf16[1,64,4096]{2,1,0:T(8,128)(2,1)} %copy.42), channel_id=1, source_target_pairs={{0,1},{1,2},{2,3},{3,4},{4,5},{5,6},{6,7},{7,0},{8,9},{9,10},{10,1... | collective-permute-start | bytes 1572872 | tf_op jit(solution)/shard_map/while/body/eval_jaxpr/ppermute | solution.py:12
  185.8 2.5 %copy-start = (f32[8]{0:T(128)S(1)}, f32[8]{0:T(128)}, u32[]{:S(2)}) copy-start(f32[8]{0:T(128)} %get-tuple-element.1191) | copy-start | bytes 100 | tf_op jit(solution)/shard_map/while
  192.7 2.5 %copy-start = (f32[8]{0:T(128)S(1)}, f32[8]{0:T(128)}, u32[]{:S(2)}) copy-start(f32[8]{0:T(128)} %get-tuple-element.1191) | copy-start | bytes 100 | tf_op jit(solution)/shard_map/while
  199.7 2.5 %copy-start = (f32[8]{0:T(128)S(1)}, f32[8]{0:T(128)}, u32[]{:S(2)}) copy-start(f32[8]{0:T(128)} %get-tuple-element.1191) | copy-start | bytes 100 | tf_op jit(solution)/shard_map/while
  206.7 2.5 %copy-start = (f32[8]{0:T(128)S(1)}, f32[8]{0:T(128)}, u32[]{:S(2)}) copy-start(f32[8]{0:T(128)} %get-tuple-element.1191) | copy-start | bytes 100 | tf_op jit(solution)/shard_map/while
Sparse Core Ops, SparseCore 0:
  9.5 51.9 all-gather.1
where the time goes:
time: 224 us; the launch traced here: 223 us
  matrix products  69.8 us (31%)
  local copies, waits for them, and re-layouts  65.9 us (29%)
  waiting for transfers between devices  45.3 us (20%)
  between operations  13.4 us (6%)
  other arithmetic  9.94 us (4%)
  blocking collectives  8.86 us (4%)
  starting transfers between devices  7.87 us (4%)
    dot_general x32, matrix products, over_sources(): jnp.einsum('gax,xm->gam', kernel_rows, density, preferred_element_type=jn...  47.2 us
    all_gather x1, waiting for transfers between devices, shards(): targets_full = lax.all_gather(targets, 'src', axis=1, tiled=True)  44.6 us
    reshape x32, local copies, waits for them, and re-layouts, over_sources(): first_pass = first_pass.reshape(term_count, row_count, side_len, side_len)  36 us
    dot_general x32, matrix products, over_sources(): jnp.einsum('gcz,gabz->abc', weighted, second_pass, preferred_element_type...  22.6 us
    dynamic_update_slice x8, local copies, waits for them, and re-layouts, over_targets(): lax.dynamic_update_slice_in_dim(summed, partial_value[:, None, :], target...  14.3 us
    all_gather x1, blocking collectives, shards(): sources_full = lax.all_gather(sources, 'tgt', axis=1, tiled=True)  8.86 us
    ppermute x7, starting transfers between devices, passed_along(): return lax.ppermute(value, axis, pairs)  7.87 us
    dynamic_slice x8, local copies, waits for them, and re-layouts, over_sources(): lax.dynamic_slice_in_dim(source, row_start, row_count, 0)  6.15 us
  transfers between devices with their start and end apart: 8, of which 1 were waited for; matrix products, arithmetic and copies ran while one was open for 49% of the time, Pallas kernels for 0%

commit v1 on v0

v1 whole, which is shorter than its diff:
```python
import functools
import math

import jax
import jax.numpy as jnp
import numpy as np
import ml_dtypes
from jax import lax
from jax.experimental import pallas as pl
from jax.experimental.pallas import tpu as pltpu
from jax.sharding import PartitionSpec as P

MESH = pl.DeviceIdType.MESH
BF16 = jnp.bfloat16
F32 = jnp.float32
YS = 8


def rounded(values):
    return values.astype(ml_dtypes.bfloat16).astype(np.float64)


@functools.lru_cache(None)
def basis(n):
    pos = np.arange(n, dtype=np.float64)
    columns, norms, freqs = [], [], []
    scales = 2.0 ** (np.arange(64) / 64)
    for k in range(n // 2 + 1):
        single = k == 0 or 2 * k == n
        best = None
        for phase in [0.0] if single else np.arange(32) * (2 * np.pi / n / 32):
            angle = 2 * np.pi * k * pos / n + phase
            pair = [np.cos(angle)] if single else [np.cos(angle), np.sin(angle)]
            for scale in scales:
                scaled = [scale * p for p in pair]
                err = sum(np.sum((rounded(p) - p) ** 2) for p in scaled) / scale**2
                if best is None or err < best[0] - 1e-15:
                    best = (err, scaled, scale)
        for p in best[1]:
            columns.append(p)
            norms.append(best[2] ** 2 * (n if single else n / 2))
            freqs.append(k)
    table = np.stack(columns, 1)
    cosines = np.cos(2 * np.pi * np.outer(np.array(freqs), pos) / n) / np.array(norms)[:, None]
    return table, cosines


def kernel(
    dims,
    tgt_ref, src_ref, exp_ref, coef_ref, cos_ref, wz_ref, wzt_ref, bx_ref, bxt_ref, by_ref, byt_ref,
    out_ref,
    sfull, tfull, s32, t32, work, spec, obuf, orecv, lam_ref, wl_ref,
    a_send, a_recv, b1_send, b1_recv, b2_send, b2_recv, b3_send, b3_recv, c_send, c_recv, local_sem,
):
    tn, sn, ni, xn, un, px, pb, m, n, nj = dims
    t = lax.axis_index("tgt")
    s = lax.axis_index("src")
    z, x = s // xn, s % xn
    u, c = t // 2, t % 2
    cn = 1 - c

    def at(tt, ss):
        return {"tgt": tt, "src": ss}

    barrier = pltpu.get_barrier_semaphore()
    for d in range(1, sn):
        pl.semaphore_signal(barrier, inc=1, device_id=at(t, (s + d) % sn), device_id_type=MESH)
    for e in range(1, un):
        pl.semaphore_signal(barrier, inc=1, device_id=at(((u + e) % un) * 2 + c, s), device_id_type=MESH)
    pl.semaphore_signal(barrier, inc=1, device_id=at(u * 2 + cn, s), device_id_type=MESH)
    pl.semaphore_wait(barrier, sn - 1 + un - 1 + 1)

    def remote(src, dst, send, recv, dev):
        return pltpu.make_async_remote_copy(
            src_ref=src, dst_ref=dst, send_sem=send, recv_sem=recv, device_id=dev, device_id_type=MESH
        )

    own_src = src_ref.at[0]
    sends = []

    def go(copy):
        copy.start()
        sends.append(copy)

    for d in range(1, ni):
        go(remote(own_src, sfull.at[z, t], b1_send.at[d], b1_recv.at[d], at(t, ((z + d) % ni) * xn + x)))
    own_copy = pltpu.make_async_copy(own_src, sfull.at[z, t], local_sem.at[0])
    own_copy.start()
    for d in range(1, sn):
        to = (s + d) % sn
        go(remote(tgt_ref.at[to // xn], tfull.at[s], a_send.at[d], a_recv.at[d], at(t, to)))
    tgt_copy = pltpu.make_async_copy(tgt_ref.at[z], tfull.at[s], local_sem.at[1])
    tgt_copy.start()

    def forward(d, block):
        src_z = (z + ni - d) % ni
        for e in range(1, un):
            go(remote(block, sfull.at[src_z, t], b2_send.at[d, e], b2_recv.at[d, e], at(((u + e) % un) * 2 + c, s)))
        go(remote(block, sfull.at[src_z, t], b3_send.at[d, 0], b3_recv.at[d, 0], at(u * 2 + cn, s)))

    forward(0, own_src)

    dist = lax.broadcasted_iota(jnp.int32, (exp_ref.shape[0], n), 1)
    dist = jnp.minimum(dist, n - dist).astype(F32)
    gauss = jnp.exp(-exp_ref[...] * (dist * dist))
    wgauss = (coef_ref[...] * gauss).astype(BF16).astype(F32)
    gauss = gauss.astype(BF16).astype(F32)
    dot = functools.partial(lax.dot_general, preferred_element_type=F32)
    hot = functools.partial(dot, precision=lax.Precision.HIGHEST)
    last = (((1,), (1,)), ((), ()))
    plain = (((1,), (0,)), ((), ()))
    lam_t = hot(cos_ref[...], gauss, last)
    lam = hot(gauss, cos_ref[...], last)
    lam_ref[...] = lam_t
    wl_ref[...] = hot(cos_ref[...], wgauss, last)
    lam_x = jnp.concatenate([lam] * nj, axis=1)
    lanes = nj * n

    def spectrum(q, carry):
        rows = wl_ref[pl.ds(pl.multiple_of(q * 8, 8), 8), :]
        left = (rows[:, None, :] * lam_ref[...][None]).reshape(8 * n, rows.shape[1])
        spec[pl.ds(pl.multiple_of(q * 8 * n, 8 * n), 8 * n), :] = hot(left, lam_x, plain)
        return carry

    lax.fori_loop(0, n // 8, spectrum, 0)

    for d in range(1, ni):
        src_z = (z + ni - d) % ni
        slot = sfull.at[src_z, t]
        remote(slot, slot, b1_send.at[d], b1_recv.at[d], at(t, s)).wait_recv()
        forward(d, slot)
    for d in range(ni):
        src_z = (z + ni - d) % ni
        for e in range(1, un):
            slot = sfull.at[src_z, ((u + un - e) % un) * 2 + c]
            remote(slot, slot, b2_send.at[d, e], b2_recv.at[d, e], at(t, s)).wait_recv()
            go(remote(slot, slot, b3_send.at[d, e], b3_recv.at[d, e], at(u * 2 + cn, s)))
    tgt_copy.wait()
    for d in range(1, sn):
        slot = tfull.at[(s + sn - d) % sn]
        remote(slot, slot, a_send.at[d], a_recv.at[d], at(t, s)).wait_recv()
    for k in range(sn):
        t32[k * px:(k + 1) * px, :] = tfull[k].astype(F32)
    own_copy.wait()
    for d in range(ni):
        src_z = (z + ni - d) % ni
        for e in range(un):
            slot = sfull.at[src_z, ((u + un - e) % un) * 2 + cn]
            remote(slot, slot, b3_send.at[d, e], b3_recv.at[d, e], at(t, s)).wait_recv()
    for j in range(nj):
        for k in range(tn):
            s32[j * n + k * pb:j * n + (k + 1) * pb, :] = sfull[j, k].astype(F32)

    width = YS * n

    def into_modes(k, carry):
        cols = pl.ds(pl.multiple_of(k * width, width), width)
        tile = t32[:, cols]
        dens = (s32[:, cols] * jnp.concatenate([tile] * nj, axis=0)).astype(BF16)
        first = dot(wz_ref[...], dens, last).astype(BF16)
        second = dot(first, bx_ref[...], plain)
        work[:, pl.ds(pl.multiple_of(k * YS, YS), YS), :] = second.reshape(n, YS, lanes)
        return carry

    lax.fori_loop(0, m // width, into_modes, 0)

    def in_modes(q, carry):
        group = pl.ds(q * nj, nj)
        rows = work[group].reshape(nj * n, lanes).astype(BF16)
        modes = dot(byt_ref[...], rows, plain)
        modes = (modes * spec[pl.ds(pl.multiple_of(q * nj * n, nj * n), nj * n), :]).astype(BF16)
        back = dot(by_ref[...], modes, plain).astype(BF16)
        back = dot(back, bxt_ref[...], plain)
        work[group] = back.reshape(nj, n, lanes)
        return carry

    lax.fori_loop(0, n // nj, in_modes, 0)

    def from_modes(k, carry):
        cols = pl.ds(pl.multiple_of(k * width, width), width)
        rows = work[:, pl.ds(pl.multiple_of(k * YS, YS), YS), :].reshape(YS * n, lanes).astype(BF16)
        pot = dot(rows, wzt_ref[...], (((0,), (0,)), ((), ())))
        prod = pot * s32[:, cols]
        total = prod[:n]
        for j in range(1, nj):
            total = total + prod[j * n:(j + 1) * n]
        total = -total
        for b in range(sn):
            obuf[b, :, cols] = total[b * px:(b + 1) * px].astype(BF16)
        return carry

    lax.fori_loop(0, m // width, from_modes, 0)

    for d in range(1, sn):
        to = (s + d) % sn
        go(remote(obuf.at[to], orecv.at[s], c_send.at[d], c_recv.at[d], at(t, to)))
    out_copy = pltpu.make_async_copy(obuf.at[s], orecv.at[s], local_sem.at[2])
    out_copy.start()
    out_copy.wait()
    for d in range(1, sn):
        slot = orecv.at[(s + sn - d) % sn]
        remote(slot, slot, c_send.at[d], c_recv.at[d], at(t, s)).wait_recv()
    for i in range(ni):
        total = orecv[i * xn].astype(F32)
        for k in range(1, xn):
            total = total + orecv[i * xn + k].astype(F32)
        out_ref[:, i, :] = total
    for copy in sends:
        copy.wait_send()


def shards(mesh_shape, targets, sources, exponents, coefficients):
    tn, sn = mesh_shape
    ni, px, m = targets.shape
    js, pb, _ = sources.shape
    n = px * sn
    xn = sn // ni
    un = tn // 2
    nj = ni * js
    assert js == 1 and m == n * n and sn % ni == 0 and tn % 2 == 0
    table, cosines = basis(n)
    eye = np.eye(YS)
    wz = np.einsum("zk,rs->krsz", table, eye).reshape(n * YS, YS * n)
    diag = np.kron(np.eye(nj), table)
    consts = [jnp.asarray(cosines, F32)] + [
        jnp.asarray(v.astype(ml_dtypes.bfloat16)) for v in (wz, wz, diag, diag.T, diag, diag.T)
    ]
    dims = (tn, sn, ni, xn, un, px, pb, m, n, nj)
    vmem = pl.BlockSpec(memory_space=pltpu.VMEM)
    gauss_count = exponents.shape[0]
    dma = pltpu.SemaphoreType.DMA
    return pl.pallas_call(
        functools.partial(kernel, dims),
        out_shape=jax.ShapeDtypeStruct((px, ni, m), F32),
        in_specs=[vmem] * 11,
        out_specs=vmem,
        scratch_shapes=[
            pltpu.VMEM((nj, tn, pb, m), BF16),
            pltpu.VMEM((sn, px, m), BF16),
            pltpu.VMEM((nj * n, m), F32),
            pltpu.VMEM((n, m), F32),
            pltpu.VMEM((n, n, nj * n), F32),
            pltpu.VMEM((n * n, nj * n), F32),
            pltpu.VMEM((sn, px, m), BF16),
            pltpu.VMEM((sn, px, m), BF16),
            pltpu.VMEM((n, gauss_count), F32),
            pltpu.VMEM((n, gauss_count), F32),
            dma((sn,)), dma((sn,)),
            dma((ni,)), dma((ni,)),
            dma((ni, un)), dma((ni, un)),
            dma((ni, un)), dma((ni, un)),
            dma((sn,)), dma((sn,)),
            dma((3,)),
        ],
        compiler_params=pltpu.CompilerParams(
            collective_id=0, has_side_effects=True, vmem_limit_bytes=48 * 1024 * 1024
        ),
    )(targets, sources, exponents[:, None], coefficients[:, None], *consts)


def solution(mesh):
    placed = (P("tgt", "src", None), P("src", "tgt", None), P(), P())
    mesh_shape = (mesh.shape["tgt"], mesh.shape["src"])
    return jax.shard_map(
        functools.partial(shards, mesh_shape),
        mesh=mesh, in_specs=placed, out_specs=P("src", "tgt", None), check_vma=False,
    )
```

time: 224 us -> 64.1 us (0.29)
  the two profiles are of different devices: /device:TPU:0 before, /device:TPU:27 now
where the time goes in v1:
time: 64.1 us; the launch traced here: 63.8 us
  Pallas kernels  56.1 us (88%)
  local copies, waits for them, and re-layouts  7.64 us (12%)
    pallas_call x1, Pallas kernels, shards(): pl.pallas_call(functools.partial(kernel, dims), out_shape=jax.ShapeDtypeS...  56.1 us
    unnamed x17, local copies, waits for them, and re-layouts  7.48 us

profile of v1, /device:TPU:27, one launch (start us, length us, event | category | flops | bytes accessed | tf_op | source)
XLA Modules:
  0.0 63.8 jit_solution(17899630439764929168)
XLA Ops:
  0.0 0.0 copy-start.6
  0.0 0.7 %copy-done.6 = f32[8]{0:T(128)S(1)} copy-done((f32[8]{0:T(128)S(1)}, f32[8]{0:T(128)}, u32[]{:S(2)}) %copy-start.6) | copy-done | bytes 56
  0.7 0.0 copy-start.7
  0.7 0.1 copy.12.exp_ref
  0.7 0.6 copy-done.7
  1.3 0.1 copy.13.coef_ref
  1.4 0.0 copy-start
  1.4 1.0 %copy-done = bf16[512,512]{1,0:T(8,128)(2,1)S(1)} copy-done((bf16[512,512]{1,0:T(8,128)(2,1)S(1)}, bf16[512,512]{1,0:T(8,128)(2,1)}, u32[]{:S(2)}) %copy-start) | copy-done | bytes 524312
  2.4 0.0 copy-start.1
  2.4 0.9 %copy-done.1 = bf16[256,256]{1,0:T(8,128)(2,1)S(1)} copy-done((bf16[256,256]{1,0:T(8,128)(2,1)S(1)}, bf16[256,256]{1,0:T(8,128)(2,1)}, u32[]{:S(2)}) %copy-start.1) | copy-done | bytes 131096
  3.3 0.0 copy-start.2
  3.3 0.9 %copy-done.2 = bf16[256,256]{1,0:T(8,128)(2,1)S(1)} copy-done((bf16[256,256]{1,0:T(8,128)(2,1)S(1)}, bf16[256,256]{1,0:T(8,128)(2,1)}, u32[]{:S(2)}) %copy-start.2) | copy-done | bytes 131096
  4.2 0.0 copy-start.3
  4.2 0.9 %copy-done.3 = bf16[4,8,4096]{2,1,0:T(8,128)(2,1)S(1)} copy-done((bf16[4,8,4096]{2,1,0:T(8,128)(2,1)S(1)}, bf16[4,8,4096]{2,1,0:T(8,128)(2,1)}, u32[]{:S(2)}) %copy-start.3) | copy-done | bytes 262168
  5.2 0.0 copy-start.4
  5.2 0.9 %copy-done.4 = bf16[1,16,4096]{2,1,0:T(8,128)(2,1)S(1)} copy-done((bf16[1,16,4096]{2,1,0:T(8,128)(2,1)S(1)}, bf16[1,16,4096]{2,1,0:T(8,128)(2,1)}, u32[]{:S(2)}) %copy-start.4) | copy-done | bytes 131096
  6.1 0.0 copy-start.5
  6.1 0.8 %copy-done.5 = f32[64,64]{1,0:T(8,128)S(1)} copy-done((f32[64,64]{1,0:T(8,128)S(1)}, f32[64,64]{1,0:T(8,128)}, u32[]{:S(2)}) %copy-start.5) | copy-done | bytes 16408
  6.9 56.1 %shard_map.109 = f32[8,4,4096]{2,1,0:T(4,128)S(1)} custom-call(bf16[4,8,4096]{2,1,0:T(8,128)(2,1)S(1)} %copy-done.3, bf16[1,16,4096]{2,1,0:T(8,128)(2,1)S(1)} %copy-done.4, f32[8,1]{1,0:T(8,128)S(1)} %copy.12.exp_ref, f32[8,1]{1,0:T(8,128)S(1)} %copy.13.coef_ref, f32[64,64]{1,0:T(8,128)S(1)} %copy-done.5, bf16[512,512]{1,0:T(8,128)(2,1)S(1)} %copy-done, ...), custom_call_target="tpu_custom_call" | custom-call | tf_op jit(solution)/shard_map/pallas_call | solution.py:232
  63.0 0.8 %copy.15 = f32[8,4,4096]{2,1,0:T(4,128)} copy(f32[8,4,4096]{2,1,0:T(4,128)S(1)} %shard_map.109) | data formatting | bytes 1048576
Async XLA Ops:
  0.0 0.7 %copy-start.6 = (f32[8]{0:T(128)S(1)}, f32[8]{0:T(128)}, u32[]{:S(2)}) copy-start(f32[8]{0:T(128)} %param.13) | copy-start | bytes 100
  0.7 0.7 %copy-start.7 = (f32[8]{0:T(128)S(1)}, f32[8]{0:T(128)}, u32[]{:S(2)}) copy-start(f32[8]{0:T(128)} %param.14) | copy-start | bytes 100
  1.4 1.0 %copy-start = (bf16[512,512]{1,0:T(8,128)(2,1)S(1)}, bf16[512,512]{1,0:T(8,128)(2,1)}, u32[]{:S(2)}) copy-start(bf16[512,512]{1,0:T(8,128)(2,1)} %constant.9.clone.wz_ref.wzt_ref) | copy-start | bytes 1572868
  2.4 0.9 %copy-start.1 = (bf16[256,256]{1,0:T(8,128)(2,1)S(1)}, bf16[256,256]{1,0:T(8,128)(2,1)}, u32[]{:S(2)}) copy-start(bf16[256,256]{1,0:T(8,128)(2,1)} %constant.11.clone.bxt_ref.byt_ref) | copy-start | bytes 393220
  3.3 0.9 %copy-start.2 = (bf16[256,256]{1,0:T(8,128)(2,1)S(1)}, bf16[256,256]{1,0:T(8,128)(2,1)}, u32[]{:S(2)}) copy-start(bf16[256,256]{1,0:T(8,128)(2,1)} %constant.10.clone.bx_ref.by_ref) | copy-start | bytes 393220
  4.2 0.9 %copy-start.3 = (bf16[4,8,4096]{2,1,0:T(8,128)(2,1)S(1)}, bf16[4,8,4096]{2,1,0:T(8,128)(2,1)}, u32[]{:S(2)}) copy-start(bf16[4,8,4096]{2,1,0:T(8,128)(2,1)} %tgt_ref.1) | copy-start | bytes 786436
  5.2 0.9 %copy-start.4 = (bf16[1,16,4096]{2,1,0:T(8,128)(2,1)S(1)}, bf16[1,16,4096]{2,1,0:T(8,128)(2,1)}, u32[]{:S(2)}) copy-start(bf16[1,16,4096]{2,1,0:T(8,128)(2,1)} %src_ref.1) | copy-start | bytes 393220
  6.1 0.8 %copy-start.5 = (f32[64,64]{1,0:T(8,128)S(1)}, f32[64,64]{1,0:T(8,128)}, u32[]{:S(2)}) copy-start(f32[64,64]{1,0:T(8,128)} %constant.8.clone.cos_ref) | copy-start | bytes 49156

commit v2 on v1

v2 whole, which is shorter than its diff:
```python
import functools
import math

import jax
import jax.numpy as jnp
import numpy as np
import ml_dtypes
from jax import lax
from jax.experimental import pallas as pl
from jax.experimental.pallas import tpu as pltpu
from jax.sharding import PartitionSpec as P

MESH = pl.DeviceIdType.MESH
BF16 = jnp.bfloat16
F32 = jnp.float32
YS = 8
PARTS = 2
CHUNKS = 4


def rounded(values):
    return values.astype(ml_dtypes.bfloat16).astype(np.float64)


@functools.lru_cache(None)
def basis(n):
    pos = np.arange(n, dtype=np.float64)
    columns, norms, freqs = [], [], []
    scales = 2.0 ** (np.arange(64) / 64)
    for k in range(n // 2 + 1):
        single = k == 0 or 2 * k == n
        best = None
        for phase in [0.0] if single else np.arange(32) * (2 * np.pi / n / 32):
            angle = 2 * np.pi * k * pos / n + phase
            pair = [np.cos(angle)] if single else [np.cos(angle), np.sin(angle)]
            for scale in scales:
                scaled = [scale * p for p in pair]
                err = sum(np.sum((rounded(p) - p) ** 2) for p in scaled) / scale**2
                if best is None or err < best[0] - 1e-15:
                    best = (err, scaled, scale)
        for p in best[1]:
            columns.append(p)
            norms.append(best[2] ** 2 * (n if single else n / 2))
            freqs.append(k)
    table = np.stack(columns, 1)
    cosines = np.cos(2 * np.pi * np.outer(np.array(freqs), pos) / n) / np.array(norms)[:, None]
    return table, cosines


def kernel(
    dims,
    tgt_ref, src_ref, exp_ref, coef_ref, cos_hbm, wz_hbm, diag_hbm, diagt_hbm,
    out_ref,
    cos_ref, wz_ref, diag_ref, diagt_ref,
    sfull, tfull, s32, t32, work, spec, acc, obuf, xrecv, zbuf, zrecv, lam_ref, wl_ref,
    a1_send, a1_recv, a2_send, a2_recv, b1_send, b1_recv, b2_send, b2_recv, b3_send, b3_recv,
    x_send, x_recv, z_send, z_recv, own_sem, const_sem,
):
    tn, sn, ni, xn, un, px, pb, m, n, nj = dims
    t = lax.axis_index("tgt")
    s = lax.axis_index("src")
    z, x = s // xn, s % xn
    u, c = t // 2, t % 2
    partner = {"tgt": u * 2 + 1 - c, "src": s}

    def z_peer(d):
        return {"tgt": t, "src": ((z + d) % ni) * xn + x}

    def x_peer(f):
        return {"tgt": t, "src": z * xn + (x + f) % xn}

    def u_peer(e):
        return {"tgt": ((u + e) % un) * 2 + c, "src": s}

    consts = [
        pltpu.make_async_copy(a, b, const_sem.at[k])
        for k, (a, b) in enumerate(
            [(cos_hbm, cos_ref), (wz_hbm, wz_ref), (diag_hbm, diag_ref), (diagt_hbm, diagt_ref)]
        )
    ]
    for copy in consts:
        copy.start()

    peers = [z_peer(d) for d in range(1, ni)] + [x_peer(f) for f in range(1, xn)]
    peers += [u_peer(e) for e in range(1, un)] + [partner]
    barrier = pltpu.get_barrier_semaphore()
    for peer in peers:
        pl.semaphore_signal(barrier, inc=1, device_id=peer, device_id_type=MESH)
    pl.semaphore_wait(barrier, len(peers))

    def remote(src, dst, send, recv, dev):
        return pltpu.make_async_remote_copy(
            src_ref=src, dst_ref=dst, send_sem=send, recv_sem=recv, device_id=dev, device_id_type=MESH
        )

    sends = []

    def go(copy):
        copy.start()
        sends.append(copy)

    def arrived(slot, send, recv):
        remote(slot, slot, send, recv, partner).wait_recv()

    part = m // PARTS

    def piece(h):
        return pl.ds(h * part, part)

    def from_z(d):
        return (z + ni - d) % ni

    def pass_source(h, d, block):
        slot = sfull.at[from_z(d), t, :, piece(h)]
        for e in range(1, un):
            go(remote(block, slot, b2_send.at[h, d, e], b2_recv.at[h, d, e], u_peer(e)))
        go(remote(block, slot, b3_send.at[h, d, 0], b3_recv.at[h, d, 0], partner))

    def pass_target(h, d, block):
        slot = tfull.at[from_z(d) * xn + x, :, piece(h)]
        for f in range(1, xn):
            go(remote(block, slot, a2_send.at[h, d, f], a2_recv.at[h, d, f], x_peer(f)))

    own = []
    for h in range(PARTS):
        src_own, tgt_own = src_ref.at[0, :, piece(h)], tgt_ref.at[z, :, piece(h)]
        for d in range(1, ni):
            go(remote(src_own, sfull.at[z, t, :, piece(h)], b1_send.at[h, d], b1_recv.at[h, d], z_peer(d)))
        for d in range(1, ni):
            go(remote(
                tgt_ref.at[(z + d) % ni, :, piece(h)], tfull.at[s, :, piece(h)],
                a1_send.at[h, d], a1_recv.at[h, d], z_peer(d),
            ))
        pass_source(h, 0, src_own)
        pass_target(h, 0, tgt_own)
        own.append(pltpu.make_async_copy(src_own, sfull.at[z, t, :, piece(h)], own_sem.at[h, 0]))
        own.append(pltpu.make_async_copy(tgt_own, tfull.at[s, :, piece(h)], own_sem.at[h, 1]))
    for copy in own:
        copy.start()

    dist = lax.broadcasted_iota(jnp.int32, (1, n), 1)
    dist = jnp.minimum(dist, n - dist).astype(F32)
    count = exp_ref.shape[0]
    gauss = jnp.concatenate([jnp.exp(-exp_ref[g] * (dist * dist)) for g in range(count)], axis=0)
    wgauss = jnp.concatenate([coef_ref[g] * gauss[g:g + 1] for g in range(count)], axis=0)
    wgauss = wgauss.astype(BF16).astype(F32)
    gauss = gauss.astype(BF16).astype(F32)
    dot = functools.partial(lax.dot_general, preferred_element_type=F32)
    hot = functools.partial(dot, precision=lax.Precision.HIGHEST)
    last = (((1,), (1,)), ((), ()))
    plain = (((1,), (0,)), ((), ()))
    for copy in consts:
        copy.wait()
    lam_ref[...] = hot(cos_ref[...], gauss, last)
    wl_ref[...] = hot(cos_ref[...], wgauss, last)
    lam = hot(gauss, cos_ref[...], last)
    lam_x = jnp.concatenate([lam] * nj, axis=1)
    lanes = nj * n
    steps = list(range(n // 8))

    def spectrum():
        if steps:
            q = steps.pop(0)
            rows = wl_ref[q * 8:(q + 1) * 8, :]
            left = (rows[:, None, :] * lam_ref[...][None]).reshape(8 * n, count)
            spec[q * 8 * n:(q + 1) * 8 * n, :] = hot(left, lam_x, plain)

    spectrum()
    for h in range(PARTS):
        for d in range(1, ni):
            slot = sfull.at[from_z(d), t, :, piece(h)]
            arrived(slot, b1_send.at[h, d], b1_recv.at[h, d])
            pass_source(h, d, slot)
            spectrum()
        for d in range(1, ni):
            slot = tfull.at[from_z(d) * xn + x, :, piece(h)]
            arrived(slot, a1_send.at[h, d], a1_recv.at[h, d])
            pass_target(h, d, slot)
    while steps:
        spectrum()
    for copy in own:
        copy.wait()

    width = YS * n

    def into_modes(k, carry):
        cols = pl.ds(pl.multiple_of(k * width, width), width)
        tile = t32[:, cols]
        dens = (s32[:, cols] * jnp.concatenate([tile] * nj, axis=0)).astype(BF16)
        first = dot(wz_ref[...], dens, last).astype(BF16)
        second = dot(first, diag_ref[...], plain)
        work[:, pl.ds(pl.multiple_of(k * YS, YS), YS), :] = second.reshape(n, YS, lanes)
        return carry

    def pass_to_partner(h):
        for d in range(ni):
            for e in range(1, un):
                slot = sfull.at[from_z(d), ((u + un - e) % un) * 2 + c, :, piece(h)]
                arrived(slot, b2_send.at[h, d, e], b2_recv.at[h, d, e])
                go(remote(slot, slot, b3_send.at[h, d, e], b3_recv.at[h, d, e], partner))

    for h in range(PARTS):
        pass_to_partner(h)
        for d in range(ni):
            for f in range(1, xn):
                slot = tfull.at[from_z(d) * xn + (x + xn - f) % xn, :, piece(h)]
                arrived(slot, a2_send.at[h, d, f], a2_recv.at[h, d, f])
        here = slice(h * part, (h + 1) * part)
        for k in range(sn):
            t32[k * px:(k + 1) * px, here] = tfull[k, :, here].astype(F32)
        for d in range(ni):
            for e in range(un):
                slot = sfull.at[from_z(d), ((u + un - e) % un) * 2 + 1 - c, :, piece(h)]
                arrived(slot, b3_send.at[h, d, e], b3_recv.at[h, d, e])
        for j in range(nj):
            for k in range(tn):
                s32[j * n + k * pb:j * n + (k + 1) * pb, here] = sfull[j, k, :, here].astype(F32)
        lax.fori_loop(h * part // width, (h + 1) * part // width, into_modes, 0, unroll=2)

    def in_modes(q, carry):
        group = pl.ds(q * nj, nj)
        rows = work[group].reshape(nj * n, lanes).astype(BF16)
        modes = dot(diagt_ref[...], rows, plain)
        modes = (modes * spec[pl.ds(pl.multiple_of(q * nj * n, nj * n), nj * n), :]).astype(BF16)
        back = dot(diag_ref[...], modes, plain).astype(BF16)
        back = dot(back, diagt_ref[...], plain)
        work[group] = back.reshape(nj, n, lanes)
        return carry

    lax.fori_loop(0, n // nj, in_modes, 0, unroll=4)

    def from_modes(k, carry):
        cols = pl.ds(pl.multiple_of(k * width, width), width)
        rows = work[:, pl.ds(pl.multiple_of(k * YS, YS), YS), :].reshape(YS * n, lanes).astype(BF16)
        pot = dot(rows, wz_ref[...], (((0,), (0,)), ((), ())))
        prod = pot * s32[:, cols]
        total = prod[:n]
        for j in range(1, nj):
            total = total + prod[j * n:(j + 1) * n]
        total = -total
        for b in range(sn):
            value = total[b * px:(b + 1) * px]
            acc[b % xn, b // xn, :, cols] = value
            obuf[b % xn, b // xn, :, cols] = value.astype(BF16)
        return carry

    chunk = m // CHUNKS

    def add_up(k):
        cols = pl.ds(k * chunk, chunk)
        for f in range(1, xn):
            arrived(xrecv.at[(x + xn - f) % xn, :, :, cols], x_send.at[k, f], x_recv.at[k, f])
        total = acc[x, :, :, cols]
        for f in range(1, xn):
            total = total + xrecv[(x + xn - f) % xn, :, :, cols].astype(F32)
        zbuf[:, :, cols] = total.astype(BF16)
        for d in range(1, ni):
            to = (z + d) % ni
            go(remote(zbuf.at[to, :, cols], zrecv.at[z, :, cols], z_send.at[k, d], z_recv.at[k, d], z_peer(d)))
        zrecv[z, :, cols] = zbuf[z, :, cols]

    for k in range(CHUNKS):
        cols = pl.ds(k * chunk, chunk)
        lax.fori_loop(k * chunk // width, (k + 1) * chunk // width, from_modes, 0, unroll=2)
        for f in range(1, xn):
            to = (x + f) % xn
            go(remote(
                obuf.at[to, :, :, cols], xrecv.at[x, :, :, cols], x_send.at[k, f], x_recv.at[k, f], x_peer(f)
            ))
        if k:
            add_up(k - 1)
    add_up(CHUNKS - 1)

    for k in range(CHUNKS):
        cols = pl.ds(k * chunk, chunk)
        for d in range(1, ni):
            arrived(zrecv.at[from_z(d), :, cols], z_send.at[k, d], z_recv.at[k, d])
        for i in range(ni):
            out_ref[:, i, cols] = zrecv[i, :, cols].astype(F32)
    for copy in sends:
        copy.wait_send()


def shards(mesh_shape, targets, sources, exponents, coefficients):
    tn, sn = mesh_shape
    ni, px, m = targets.shape
    js, pb, _ = sources.shape
    n = px * sn
    xn = sn // ni
    un = tn // 2
    nj = ni * js
    assert js == 1 and m == n * n and sn % ni == 0 and tn % 2 == 0
    table, cosines = basis(n)
    wz = np.einsum("zk,rs->krsz", table, np.eye(YS)).reshape(n * YS, YS * n)
    diag = np.kron(np.eye(nj), table)
    consts = [jnp.asarray(cosines, F32)] + [
        jnp.asarray(v.astype(ml_dtypes.bfloat16)) for v in (wz, diag, diag.T)
    ]
    dims = (tn, sn, ni, xn, un, px, pb, m, n, nj)
    anywhere = pl.BlockSpec(memory_space=pl.ANY)
    scalars = pl.BlockSpec(memory_space=pltpu.SMEM)
    gauss_count = exponents.shape[0]
    dma = pltpu.SemaphoreType.DMA

    def pair(*shape):
        return [dma(shape), dma(shape)]

    return pl.pallas_call(
        functools.partial(kernel, dims),
        out_shape=jax.ShapeDtypeStruct((px, ni, m), F32),
        in_specs=[anywhere, anywhere, scalars, scalars] + [anywhere] * 4,
        out_specs=pl.BlockSpec(memory_space=pltpu.VMEM),
        scratch_shapes=[
            pltpu.VMEM(consts[0].shape, F32),
            *[pltpu.VMEM(v.shape, BF16) for v in consts[1:]],
            pltpu.VMEM((nj, tn, pb, m), BF16),
            pltpu.VMEM((sn, px, m), BF16),
            pltpu.VMEM((nj * n, m), F32),
            pltpu.VMEM((n, m), F32),
            pltpu.VMEM((n, n, nj * n), F32),
            pltpu.VMEM((n * n, nj * n), F32),
            pltpu.VMEM((xn, ni, px, m), F32),
            pltpu.VMEM((xn, ni, px, m), BF16),
            pltpu.VMEM((xn, ni, px, m), BF16),
            pltpu.VMEM((ni, px, m), BF16),
            pltpu.VMEM((ni, px, m), BF16),
            pltpu.VMEM((n, gauss_count), F32),
            pltpu.VMEM((n, gauss_count), F32),
            *pair(PARTS, ni), *pair(PARTS, ni, xn),
            *pair(PARTS, ni), *pair(PARTS, ni, un), *pair(PARTS, ni, un),
            *pair(CHUNKS, xn), *pair(CHUNKS, ni),
            dma((PARTS, 2)), dma((4,)),
        ],
        compiler_params=pltpu.CompilerParams(
            collective_id=0, has_side_effects=True, vmem_limit_bytes=48 * 1024 * 1024
        ),
    )(targets, sources, exponents, coefficients, *consts)


def solution(mesh):
    placed = (P("tgt", "src", None), P("src", "tgt", None), P(), P())
    mesh_shape = (mesh.shape["tgt"], mesh.shape["src"])
    return jax.shard_map(
        functools.partial(shards, mesh_shape),
        mesh=mesh, in_specs=placed, out_specs=P("src", "tgt", None), check_vma=False,
    )
```

time: 64.1 us -> 59.9 us (0.934)
  the two profiles are of different devices: /device:TPU:27 before, /device:TPU:0 now
where the time goes in v2:
time: 59.9 us; the launch traced here: 59.5 us
  Pallas kernels  51.9 us (87%)
  local copies, waits for them, and re-layouts  7.56 us (13%)
    pallas_call x1, Pallas kernels, shards(): pl.pallas_call(functools.partial(kernel, dims), out_shape=jax.ShapeDtypeS...  51.9 us
    unnamed x17, local copies, waits for them, and re-layouts  7.56 us

profile of v2, /device:TPU:0, one launch (start us, length us, event | category | flops | bytes accessed | tf_op | source)
XLA Modules:
  0.0 59.5 jit_solution(5629322696486613744)
XLA Ops:
  0.0 0.0 copy-start
  0.0 1.0 %copy-done = bf16[512,512]{1,0:T(8,128)(2,1)S(1)} copy-done((bf16[512,512]{1,0:T(8,128)(2,1)S(1)}, bf16[512,512]{1,0:T(8,128)(2,1)}, u32[]{:S(2)}) %copy-start) | copy-done | bytes 524312
  1.0 0.0 copy-start.1
  1.0 0.9 %copy-done.1 = bf16[4,8,4096]{2,1,0:T(8,128)(2,1)S(1)} copy-done((bf16[4,8,4096]{2,1,0:T(8,128)(2,1)S(1)}, bf16[4,8,4096]{2,1,0:T(8,128)(2,1)}, u32[]{:S(2)}) %copy-start.1) | copy-done | bytes 262168
  2.0 0.0 copy-start.2
  2.0 0.9 %copy-done.2 = bf16[1,16,4096]{2,1,0:T(8,128)(2,1)S(1)} copy-done((bf16[1,16,4096]{2,1,0:T(8,128)(2,1)S(1)}, bf16[1,16,4096]{2,1,0:T(8,128)(2,1)}, u32[]{:S(2)}) %copy-start.2) | copy-done | bytes 131096
  2.9 0.0 copy-start.3
  2.9 0.9 %copy-done.3 = bf16[256,256]{1,0:T(8,128)(2,1)S(1)} copy-done((bf16[256,256]{1,0:T(8,128)(2,1)S(1)}, bf16[256,256]{1,0:T(8,128)(2,1)}, u32[]{:S(2)}) %copy-start.3) | copy-done | bytes 131096
  3.8 0.0 copy-start.4
  3.8 0.9 %copy-done.4 = bf16[256,256]{1,0:T(8,128)(2,1)S(1)} copy-done((bf16[256,256]{1,0:T(8,128)(2,1)S(1)}, bf16[256,256]{1,0:T(8,128)(2,1)}, u32[]{:S(2)}) %copy-start.4) | copy-done | bytes 131096
  4.7 0.0 copy-start.5
  4.7 0.8 %copy-done.5 = f32[64,64]{1,0:T(8,128)S(1)} copy-done((f32[64,64]{1,0:T(8,128)S(1)}, f32[64,64]{1,0:T(8,128)}, u32[]{:S(2)}) %copy-start.5) | copy-done | bytes 16408
  5.5 0.0 copy-start.6
  5.5 0.7 %copy-done.6 = f32[8]{0:T(128)S(1)} copy-done((f32[8]{0:T(128)S(1)}, f32[8]{0:T(128)}, u32[]{:S(2)}) %copy-start.6) | copy-done | bytes 56
  6.1 0.0 copy-start.7
  6.1 0.7 %copy-done.7 = f32[8]{0:T(128)S(1)} copy-done((f32[8]{0:T(128)S(1)}, f32[8]{0:T(128)}, u32[]{:S(2)}) %copy-start.7) | copy-done | bytes 56
  6.8 51.9 %shard_map.82 = f32[8,4,4096]{2,1,0:T(4,128)S(1)} custom-call(bf16[4,8,4096]{2,1,0:T(8,128)(2,1)S(1)} %copy-done.1, bf16[1,16,4096]{2,1,0:T(8,128)(2,1)S(1)} %copy-done.2, f32[8]{0:T(128)S(1)} %copy-done.6, f32[8]{0:T(128)S(1)} %copy-done.7, f32[64,64]{1,0:T(8,128)S(1)} %copy-done.5, bf16[512,512]{1,0:T(8,128)(2,1)S(1)} %copy-done, ...), custom_call_target="tpu_custom_call" | custom-call | tf_op jit(solution)/shard_map/pallas_call | solution.py:308
  58.7 0.8 %copy.10 = f32[8,4,4096]{2,1,0:T(4,128)} copy(f32[8,4,4096]{2,1,0:T(4,128)S(1)} %shard_map.82) | data formatting | bytes 1048576
Async XLA Ops:
  0.0 1.0 %copy-start = (bf16[512,512]{1,0:T(8,128)(2,1)S(1)}, bf16[512,512]{1,0:T(8,128)(2,1)}, u32[]{:S(2)}) copy-start(bf16[512,512]{1,0:T(8,128)(2,1)} %constant.9.clone.wz_hbm) | copy-start | bytes 1572868
  1.0 0.9 %copy-start.1 = (bf16[4,8,4096]{2,1,0:T(8,128)(2,1)S(1)}, bf16[4,8,4096]{2,1,0:T(8,128)(2,1)}, u32[]{:S(2)}) copy-start(bf16[4,8,4096]{2,1,0:T(8,128)(2,1)} %tgt_ref.1) | copy-start | bytes 786436
  2.0 0.9 %copy-start.2 = (bf16[1,16,4096]{2,1,0:T(8,128)(2,1)S(1)}, bf16[1,16,4096]{2,1,0:T(8,128)(2,1)}, u32[]{:S(2)}) copy-start(bf16[1,16,4096]{2,1,0:T(8,128)(2,1)} %src_ref.1) | copy-start | bytes 393220
  2.9 0.9 %copy-start.3 = (bf16[256,256]{1,0:T(8,128)(2,1)S(1)}, bf16[256,256]{1,0:T(8,128)(2,1)}, u32[]{:S(2)}) copy-start(bf16[256,256]{1,0:T(8,128)(2,1)} %constant.11.clone.diagt_hbm) | copy-start | bytes 393220
  3.8 0.9 %copy-start.4 = (bf16[256,256]{1,0:T(8,128)(2,1)S(1)}, bf16[256,256]{1,0:T(8,128)(2,1)}, u32[]{:S(2)}) copy-start(bf16[256,256]{1,0:T(8,128)(2,1)} %constant.10.clone.diag_hbm) | copy-start | bytes 393220
  4.7 0.8 %copy-start.5 = (f32[64,64]{1,0:T(8,128)S(1)}, f32[64,64]{1,0:T(8,128)}, u32[]{:S(2)}) copy-start(f32[64,64]{1,0:T(8,128)} %constant.8.clone.cos_hbm) | copy-start | bytes 49156
  5.5 0.7 %copy-start.6 = (f32[8]{0:T(128)S(1)}, f32[8]{0:T(128)}, u32[]{:S(2)}) copy-start(f32[8]{0:T(128)} %exp_ref.1) | copy-start | bytes 100
  6.1 0.7 %copy-start.7 = (f32[8]{0:T(128)S(1)}, f32[8]{0:T(128)}, u32[]{:S(2)}) copy-start(f32[8]{0:T(128)} %coef_ref.1) | copy-start | bytes 100

commit v3 on v2

--- a/solution.py
+++ b/solution.py
@@ -63,8 +63,14 @@
     u, c = t // 2, t % 2
     partner = {"tgt": u * 2 + 1 - c, "src": s}
 
+    def across(d):
+        to = z
+        for bit in [1 << k for k in range(ni.bit_length()) if d >> k & 1]:
+            to = to + bit - 2 * bit * (z // bit % 2)
+        return to
+
     def z_peer(d):
-        return {"tgt": t, "src": ((z + d) % ni) * xn + x}
+        return {"tgt": t, "src": across(d) * xn + x}
 
     def x_peer(f):
         return {"tgt": t, "src": z * xn + (x + f) % xn}
@@ -107,17 +113,19 @@
     def piece(h):
         return pl.ds(h * part, part)
 
-    def from_z(d):
-        return (z + ni - d) % ni
+    def hand_on(h, d, bit, block):
+        r = d ^ bit
+        slot = sfull.at[across(d), t, :, piece(h)]
+        go(remote(block, slot, b1_send.at[h, r], b1_recv.at[h, r], z_peer(bit)))
 
     def pass_source(h, d, block):
-        slot = sfull.at[from_z(d), t, :, piece(h)]
+        slot = sfull.at[across(d), t, :, piece(h)]
         for e in range(1, un):
             go(remote(block, slot, b2_send.at[h, d, e], b2_recv.at[h, d, e], u_peer(e)))
         go(remote(block, slot, b3_send.at[h, d, 0], b3_recv.at[h, d, 0], partner))
 
     def pass_target(h, d, block):
-        slot = tfull.at[from_z(d) * xn + x, :, piece(h)]
+        slot = tfull.at[across(d) * xn + x, :, piece(h)]
         for f in range(1, xn):
             go(remote(block, slot, a2_send.at[h, d, f], a2_recv.at[h, d, f], x_peer(f)))
 
@@ -125,10 +133,11 @@
     for h in range(PARTS):
         src_own, tgt_own = src_ref.at[0, :, piece(h)], tgt_ref.at[z, :, piece(h)]
         for d in range(1, ni):
-            go(remote(src_own, sfull.at[z, t, :, piece(h)], b1_send.at[h, d], b1_recv.at[h, d], z_peer(d)))
+            if d & (d - 1) == 0:
+                hand_on(h, 0, d, src_own)
         for d in range(1, ni):
             go(remote(
-                tgt_ref.at[(z + d) % ni, :, piece(h)], tfull.at[s, :, piece(h)],
+                tgt_ref.at[across(d), :, piece(h)], tfull.at[s, :, piece(h)],
                 a1_send.at[h, d], a1_recv.at[h, d], z_peer(d),
             ))
         pass_source(h, 0, src_own)
@@ -167,13 +176,15 @@
 
     spectrum()
     for h in range(PARTS):
-        for d in range(1, ni):
-            slot = sfull.at[from_z(d), t, :, piece(h)]
+        for d in sorted(range(1, ni), key=lambda r: -(r & -r)):
+            slot = sfull.at[across(d), t, :, piece(h)]
             arrived(slot, b1_send.at[h, d], b1_recv.at[h, d])
+            for bit in [1 << k for k in range(ni.bit_length()) if 1 << k < (d & -d)]:
+                hand_on(h, d, bit, slot)
             pass_source(h, d, slot)
             spectrum()
         for d in range(1, ni):
-            slot = tfull.at[from_z(d) * xn + x, :, piece(h)]
+            slot = tfull.at[across(d) * xn + x, :, piece(h)]
             arrived(slot, a1_send.at[h, d], a1_recv.at[h, d])
             pass_target(h, d, slot)
     while steps:
@@ -195,7 +206,7 @@
     def pass_to_partner(h):
         for d in range(ni):
             for e in range(1, un):
-                slot = sfull.at[from_z(d), ((u + un - e) % un) * 2 + c, :, piece(h)]
+                slot = sfull.at[across(d), ((u + un - e) % un) * 2 + c, :, piece(h)]
                 arrived(slot, b2_send.at[h, d, e], b2_recv.at[h, d, e])
                 go(remote(slot, slot, b3_send.at[h, d, e], b3_recv.at[h, d, e], partner))
 
@@ -203,14 +214,14 @@
         pass_to_partner(h)
         for d in range(ni):
             for f in range(1, xn):
-                slot = tfull.at[from_z(d) * xn + (x + xn - f) % xn, :, piece(h)]
+                slot = tfull.at[across(d) * xn + (x + xn - f) % xn, :, piece(h)]
                 arrived(slot, a2_send.at[h, d, f], a2_recv.at[h, d, f])
         here = slice(h * part, (h + 1) * part)
         for k in range(sn):
             t32[k * px:(k + 1) * px, here] = tfull[k, :, here].astype(F32)
         for d in range(ni):
             for e in range(un):
-                slot = sfull.at[from_z(d), ((u + un - e) % un) * 2 + 1 - c, :, piece(h)]
+                slot = sfull.at[across(d), ((u + un - e) % un) * 2 + 1 - c, :, piece(h)]
                 arrived(slot, b3_send.at[h, d, e], b3_recv.at[h, d, e])
         for j in range(nj):
             for k in range(tn):
@@ -255,7 +266,7 @@
             total = total + xrecv[(x + xn - f) % xn, :, :, cols].astype(F32)
         zbuf[:, :, cols] = total.astype(BF16)
         for d in range(1, ni):
-            to = (z + d) % ni
+            to = across(d)
             go(remote(zbuf.at[to, :, cols], zrecv.at[z, :, cols], z_send.at[k, d], z_recv.at[k, d], z_peer(d)))
         zrecv[z, :, cols] = zbuf[z, :, cols]
 
@@ -274,7 +285,7 @@
     for k in range(CHUNKS):
         cols = pl.ds(k * chunk, chunk)
         for d in range(1, ni):
-            arrived(zrecv.at[from_z(d), :, cols], z_send.at[k, d], z_recv.at[k, d])
+            arrived(zrecv.at[across(d), :, cols], z_send.at[k, d], z_recv.at[k, d])
         for i in range(ni):
             out_ref[:, i, cols] = zrecv[i, :, cols].astype(F32)
     for copy in sends:
@@ -289,7 +300,7 @@
     xn = sn // ni
     un = tn // 2
     nj = ni * js
-    assert js == 1 and m == n * n and sn % ni == 0 and tn % 2 == 0
+    assert js == 1 and m == n * n and sn % ni == 0 and ni & (ni - 1) == 0 and tn % 2 == 0
     table, cosines = basis(n)
     wz = np.einsum("zk,rs->krsz", table, np.eye(YS)).reshape(n * YS, YS * n)
     diag = np.kron(np.eye(nj), table)
@@ -297,7 +308,7 @@
         jnp.asarray(v.astype(ml_dtypes.bfloat16)) for v in (wz, diag, diag.T)
     ]
     dims = (tn, sn, ni, xn, un, px, pb, m, n, nj)
-    anywhere = pl.BlockSpec(memory_space=pl.ANY)
+    anywhere = pl.BlockSpec(memory_space=pltpu.HBM)
     scalars = pl.BlockSpec(memory_space=pltpu.SMEM)
     gauss_count = exponents.shape[0]
     dma = pltpu.SemaphoreType.DMA
@@ -332,7 +343,7 @@
             dma((PARTS, 2)), dma((4,)),
         ],
         compiler_params=pltpu.CompilerParams(
-            collective_id=0, has_side_effects=True, vmem_limit_bytes=48 * 1024 * 1024
+            collective_id=0, has_side_effects=True, vmem_limit_bytes=62 * 1024 * 1024
         ),
     )(targets, sources, exponents, coefficients, *consts)
 

time: 59.9 us -> 53.6 us (0.89)
  local copies, waits for them, and re-layouts: 7.56 us -> 1.87 us
    unnamed x17 -> x1, local copies, waits for them, and re-layouts: 7.56 us -> 1.87 us
where the time goes in v3:
time: 53.6 us; the launch traced here: 53.4 us
  Pallas kernels  51.5 us (96%)
  local copies, waits for them, and re-layouts  1.87 us (3%)
    pallas_call x1, Pallas kernels, shards(): pl.pallas_call(functools.partial(kernel, dims), out_shape=jax.ShapeDtypeS...  51.5 us
    unnamed x1, local copies, waits for them, and re-layouts  1.87 us

profile of v3, /device:TPU:0, one launch (start us, length us, event | category | flops | bytes accessed | tf_op | source)
XLA Modules:
  0.0 53.4 jit_solution(79545112180010932)
XLA Ops:
  0.0 51.5 %shard_map.82 = f32[8,4,4096]{2,1,0:T(4,128)} custom-call(bf16[4,8,4096]{2,1,0:T(8,128)(2,1)} %tgt_ref.1, bf16[1,16,4096]{2,1,0:T(8,128)(2,1)} %src_ref.1, f32[8]{0:T(128)} %exp_ref.1, f32[8]{0:T(128)} %coef_ref.1, f32[64,64]{1,0:T(8,128)} %constant.8.clone.cos_hbm, bf16[512,512]{1,0:T(8,128)(2,1)} %constant.9.clone.wz_hbm, ...), custom_call_target="tpu_custom_call" | custom-call | tf_op jit(solution)/shard_map/pallas_call | solution.py:319
  51.5 1.9 %copy.10 = f32[8,4,4096]{2,1,0:T(4,128)} copy(f32[8,4,4096]{2,1,0:T(4,128)} %shard_map.82) | data formatting | bytes 1048576
